TPU v7x, 32 devices: a whole 2x2x4 slice. The times are simulated.
32 devices in a mesh: grp: 2 (over x), row: 8 (over z, y), col: 2 (over core).
Axes of the slice: x: 2, y: 2, z: 4, core: 2. Of those that a mesh axis runs over, the one named last changes fastest.
Arguments:
- x_codes: bfloat16 [4096, 16384], P(('grp', 'col'), 'row'), parts along dimension 0, may hold values from -6 to 6
- x_scale: bfloat16 [4096, 128], P(('grp', 'col'), 'row'), parts along dimension 0, may hold values from 0.5 to 2
- grad_codes: bfloat16 [4096, 16384], P(('grp', 'col'), 'row'), parts along dimension 0, may hold values from -6 to 6
- grad_scale: bfloat16 [4096, 128], P(('grp', 'col'), 'row'), parts along dimension 0, may hold values from 0.5 to 2
- gate_pre: bfloat16 [4096, 2048], P(('grp', 'row'), 'col'), parts along dimension 0, may hold values from -6 to 6
- up_pre: bfloat16 [4096, 2048], P(('grp', 'row'), 'col'), parts along dimension 0, may hold values from -6 to 6
- w_gate: bfloat16 [16384, 2048], P('row', 'col'), may hold values from -0.046875 to 0.046875
- gate_scale: float32 [128, 16], P('row', 'col'), may hold values from 0.5 to 2
- w_up: bfloat16 [16384, 2048], P('row', 'col'), may hold values from -0.046875 to 0.046875
- up_scale: float32 [128, 16], P('row', 'col'), may hold values from 0.5 to 2
- w_down: bfloat16 [2048, 16384], P('col', 'row'), may hold values from -0.125 to 0.125
- down_scale: float32 [16, 128], P('col', 'row'), may hold values from 0.5 to 2
Outputs:
- grad_input: bfloat16 [4096, 16384], P(('grp', 'col'), 'row'), parts along dimension 0
- grad_gate: bfloat16 [32768, 2048], P(('grp', 'row'), 'col'), parts along dimension 0
- grad_up: bfloat16 [32768, 2048], P(('grp', 'row'), 'col'), parts along dimension 0
- grad_down: bfloat16 [4096, 16384], P(('grp', 'col'), 'row'), parts along dimension 0
There are 2 independent parts, one for each index of `grp`. A program takes and returns all parts, laid end to end along the dimension named above; an argument that names none is the same for every part. Nothing has to cross between parts.
All inputs are finite; a program needn't handle non-finite values.
Results may differ from a plain program's by a relative error of at most 0.007.
Values may be sent and summed in bfloat16 or wider, within the bound.
A program may use at most 256 MiB of HBM per device.

v0:
```python
import jax
import jax.numpy as jnp
from jax import lax
from jax.sharding import PartitionSpec as P

block_edge = 128


def rows_dequant(codes, scale):
    count, width = codes.shape
    parts = codes.astype(jnp.float32).reshape(count, width // block_edge, block_edge)
    return (
        (parts * scale.astype(jnp.float32)[:, :, None]).reshape(count, width).astype(jnp.bfloat16)
    )


def tile_dequant(codes, scale):
    height, width = codes.shape
    parts = codes.astype(jnp.float32).reshape(
        height // block_edge, block_edge, width // block_edge, block_edge
    )
    return (parts * scale[:, None, :, None]).reshape(height, width).astype(jnp.bfloat16)


def swiglu_back(hidden_grad, gate_pre, up_pre):
    gate_val = gate_pre.astype(jnp.float32)
    up_val = up_pre.astype(jnp.float32)
    sigma = jax.nn.sigmoid(gate_val)
    active = gate_val * sigma
    hidden = (active * up_val).astype(jnp.bfloat16)
    up_grad = (hidden_grad * active).astype(jnp.bfloat16)
    gate_grad = (hidden_grad * up_val * sigma * (1.0 + gate_val * (1.0 - sigma))).astype(
        jnp.bfloat16
    )
    return (hidden, gate_grad, up_grad)


def local(
    x_codes,
    x_scale,
    grad_codes,
    grad_scale,
    gate_pre,
    up_pre,
    w_gate,
    gate_scale,
    w_up,
    up_scale,
    w_down,
    down_scale,
):
    inner = (((1,), (1,)), ((), ()))
    outer = (((0,), (0,)), ((), ()))
    all_grad_codes, all_grad_scale, all_x_codes, all_x_scale = (
        lax.all_gather(grad_codes, "col", axis=0, tiled=True),
        lax.all_gather(grad_scale, "col", axis=0, tiled=True),
        lax.all_gather(x_codes, "col", axis=0, tiled=True),
        lax.all_gather(x_scale, "col", axis=0, tiled=True),
    )
    out_grad = rows_dequant(all_grad_codes, all_grad_scale)
    inputs = rows_dequant(all_x_codes, all_x_scale)
    gate_full = tile_dequant(w_gate, gate_scale)
    up_full = tile_dequant(w_up, up_scale)
    down_full = tile_dequant(w_down, down_scale)
    hidden_part = lax.psum_scatter(
        lax.dot_general(out_grad, down_full, inner, preferred_element_type=jnp.float32),
        "row",
        scatter_dimension=0,
        tiled=True,
    )
    hidden_mine, gate_mine, up_mine = swiglu_back(hidden_part, gate_pre, up_pre)
    hidden, gate_grad, up_grad = (
        lax.all_gather(hidden_mine, "row", axis=0, tiled=True),
        lax.all_gather(gate_mine, "row", axis=0, tiled=True),
        lax.all_gather(up_mine, "row", axis=0, tiled=True),
    )
    total = lax.dot_general(gate_grad, gate_full, inner, preferred_element_type=jnp.float32)
    grad_input = lax.psum_scatter(
        total + lax.dot_general(up_grad, up_full, inner, preferred_element_type=jnp.float32),
        "col",
        scatter_dimension=0,
        tiled=True,
    )
    factor = jnp.float32(1.0) / jnp.sqrt(jnp.float32(inputs.shape[0]))
    grad_gate = (
        lax.dot_general(inputs, gate_grad, outer, preferred_element_type=jnp.float32) * factor
    )
    grad_up = lax.dot_general(inputs, up_grad, outer, preferred_element_type=jnp.float32) * factor
    grad_down = (
        lax.dot_general(hidden, out_grad, outer, preferred_element_type=jnp.float32) * factor
    )
    return (
        grad_input.astype(jnp.bfloat16),
        grad_gate.astype(jnp.bfloat16),
        grad_up.astype(jnp.bfloat16),
        grad_down.astype(jnp.bfloat16),
    )


def solution(mesh):
    return jax.shard_map(
        local,
        mesh=mesh,
        in_specs=(
            P(("grp", "col"), "row"),
            P(("grp", "col"), "row"),
            P(("grp", "col"), "row"),
            P(("grp", "col"), "row"),
            P(("grp", "row"), "col"),
            P(("grp", "row"), "col"),
            P("row", "col"),
            P("row", "col"),
            P("row", "col"),
            P("row", "col"),
            P("col", "row"),
            P("col", "row"),
        ),
        out_specs=(
            P(("grp", "col"), "row"),
            P(("grp", "row"), "col"),
            P(("grp", "row"), "col"),
            P(("grp", "col"), "row"),
        ),
        check_vma=False,
    )
```

profile of v0, /device:TPU:0, one launch (start us, length us, event | category | flops | bytes accessed | tf_op | source)
XLA Modules:
  0.0 512.5 jit_solution(13074478246629874604)
XLA Ops:
  7.2 0.7 all-gather.6.cloned.1.call-update
  7.9 2.4 all_gather.22
  10.3 0.2 copy.16
  10.5 21.6 %all-gather.6.cloned.1.call-done = bf16[2048,2048]{1,0:T(8,128)(2,1)} async-done(((bf16[1024,2048]{1,0:T(8,128)(2,1)}), bf16[2048,2048]{1,0:T(8,128)(2,1)}) %all-gather.6.cloned.1.call-update) | async-done | bytes 8388624 | tf_op jit(solution)/shard_map/all_gather | solution.py:55
  32.1 9.0 %mul.88 = f32[2048,16,128]{2,1,0:T(8,128)} broadcast(f32[2048,16]{1,0:T(8,128)S(1)} %copy.16), dimensions={0,1} | broadcast | bytes 16908288 | tf_op jit(solution)/shard_map/mul | solution.py:13
  41.1 3.9 mul.91
  44.9 30.0 %fusion.5 = f32[2048,1024]{1,0:T(8,128)} fusion(f32[128,8,16,128]{3,2,1,0:T(8,128)} %bitcast.46, bf16[1024,2048]{1,0:T(8,128)(2,1)} %param.22, f32[256,8,16,128]{3,2,1,0:T(8,128)} %bitcast.40, bf16[2048,2048]{1,0:T(8,128)(2,1)} %all-gather.6.cloned.1.call-done), kind=kOutput, calls=%fused_computation.14 | convolution fusion | flops 8608808960 | bytes 46137344 | tf_op jit(solution)/shard_map/dot_general | solution.py:66
  75.1 150.4 %reduce-scatter.3.cloned.1.call-done = f32[256,1024]{1,0:T(8,128)} async-done(((f32[2048,1024]{1,0:T(8,128)}), f32[256,1024]{1,0:T(8,128)}) %reduce-scatter.3.cloned.1.call-update) | async-done | bytes 1048592 | tf_op jit(solution)/shard_map/reduce_scatter | solution.py:65
  225.4 3.0 multiply_convert_fusion.3
  228.5 0.5 all-gather.10.cloned.1.call-update
  229.1 0.5 all-gather.12.cloned.1.call-update
  229.7 0.5 all-gather.14.cloned.1.call-update
  230.2 0.3 reduce-scatter.5.cloned.1.call-start
  230.5 0.1 copy.17
  230.6 0.1 copy.18
  230.7 70.3 %all-gather.8.cloned.1.call-done = bf16[2048,1024]{1,0:T(8,128)(2,1)} async-done(((bf16[256,1024]{1,0:T(8,128)(2,1)}), bf16[2048,1024]{1,0:T(8,128)(2,1)}) %all-gather.8.cloned.1.call-update) | async-done | bytes 4194320 | tf_op jit(solution)/shard_map/all_gather | solution.py:74
  301.0 0.6 mul.98
  301.6 1.6 copy-done.7
  303.2 14.1 %fusion.7 = f32[2048,2048]{1,0:T(8,128)} fusion(bf16[2048,1024]{1,0:T(8,128)(2,1)} %all-gather.8.cloned.1.call-done, f32[256,8,8,128]{3,2,1,0:T(8,128)S(1)} %bitcast.45, bf16[2048,1024]{1,0:T(8,128)(2,1)S(1)} %copy-done.7), kind=kOutput, calls=%fused_computation.15 | convolution fusion | flops 8596226048 | bytes 33554432 | tf_op jit(solution)/shard_map/dot_general | solution.py:77
  317.3 58.2 %all-gather.10.cloned.1.call-done = bf16[2048,1024]{1,0:T(8,128)(2,1)} async-done(((bf16[256,1024]{1,0:T(8,128)(2,1)}), bf16[2048,1024]{1,0:T(8,128)(2,1)}) %all-gather.10.cloned.1.call-update) | async-done | bytes 4194320 | tf_op jit(solution)/shard_map/all_gather | solution.py:75
  375.5 3.8 mul.103
  379.3 22.7 %convolution_add_fusion = f32[2048,2048]{1,0:T(8,128)} fusion(f32[2048,2048]{1,0:T(8,128)} %fusion.7, bf16[2048,1024]{1,0:T(8,128)(2,1)} %all-gather.10.cloned.1.call-done, f32[256,8,8,128]{3,2,1,0:T(8,128)} %bitcast.44, bf16[2048,1024]{1,0:T(8,128)(2,1)} %param.20), kind=kOutput, calls=%fused_computation.13 | convolution fusion | flops 8600420352 | bytes 50331648 | tf_op jit(solution)/shard_map/dot_general | solution.py:79
  402.1 0.7 copy-done.2
  402.8 1.8 all_gather.26
  404.6 0.2 copy.19
  404.9 9.0 %mul.106 = f32[2048,16,128]{2,1,0:T(8,128)} broadcast(f32[2048,16]{1,0:T(8,128)S(1)} %copy.19), dimensions={0,1} | broadcast | bytes 16908288 | tf_op jit(solution)/shard_map/mul | solution.py:13
  413.9 19.4 %multiply_convert_fusion.1 = bf16[2048,1024]{1,0:T(8,128)(2,1)} fusion(bf16[2048,1024]{1,0:T(8,128)(2,1)} %all-gather.10.cloned.1.call-done, f32[256,8,16,128]{3,2,1,0:T(8,128)} %bitcast.42, bf16[2048,2048]{1,0:T(8,128)(2,1)S(1)} %copy-done.6), kind=kOutput, calls=%fused_computation.11 | convolution fusion | flops 8606711808 | bytes 33554432 | tf_op jit(solution)/shard_map/dot_general | solution.py:88
  433.4 26.1 %multiply_convert_fusion.2 = bf16[2048,1024]{1,0:T(8,128)(2,1)} fusion(bf16[2048,1024]{1,0:T(8,128)(2,1)S(1)} %copy-done.8, f32[256,8,16,128]{3,2,1,0:T(8,128)} %bitcast.43, bf16[2048,2048]{1,0:T(8,128)(2,1)S(1)} %copy-done.6), kind=kOutput, calls=%fused_computation.12 | convolution fusion | flops 8606711808 | bytes 33554432 | tf_op jit(solution)/shard_map/dot_general | solution.py:86
  459.5 13.0 %all-gather.14.cloned.1.call-done = bf16[2048,1024]{1,0:T(8,128)(2,1)} async-done(((bf16[256,1024]{1,0:T(8,128)(2,1)}), bf16[2048,1024]{1,0:T(8,128)(2,1)}) %all-gather.14.cloned.1.call-update) | async-done | bytes 4194320 | tf_op jit(solution)/shard_map/all_gather | solution.py:73
  472.5 17.2 %multiply_convert_fusion = bf16[1024,2048]{1,0:T(8,128)(2,1)} fusion(bf16[2048,1024]{1,0:T(8,128)(2,1)} %all-gather.14.cloned.1.call-done, f32[256,8,16,128]{3,2,1,0:T(8,128)} %bitcast.41, bf16[2048,2048]{1,0:T(8,128)(2,1)} %all-gather.6.cloned.1.call-done), kind=kOutput, calls=%fused_computation.10 | convolution fusion | flops 8606711808 | bytes 33554432 | tf_op jit(solution)/shard_map/dot_general | solution.py:90
  489.7 9.8 %reduce-scatter.5.cloned.1.call-done = f32[1024,2048]{1,0:T(8,128)} async-done(((f32[2048,2048]{1,0:T(8,128)}), f32[1024,2048]{1,0:T(8,128)}) %reduce-scatter.5.cloned.1.call-update) | async-done | bytes 8388624 | tf_op jit(solution)/shard_map/reduce_scatter | solution.py:78
  499.4 6.0 %convert_element_type.76 = bf16[1024,2048]{1,0:T(8,128)(2,1)} convert(f32[1024,2048]{1,0:T(8,128)} %reduce-scatter.5.cloned.1.call-done) | non-fusion elementwise | flops 2097152 | bytes 12582912 | tf_op jit(solution)/shard_map/convert_element_type | solution.py:93
  (26 shorter events, 0.3 us)
Async XLA Ops:
  7.2 25.0 %all-gather.6.cloned.1.call-start = ((), (), s32[]{:S(2)}) async-start(), calls=%async_computation.2 | async-start | bytes 12582912 | tf_op jit(solution)/shard_map/all_gather | solution.py:55
  7.9 217.5 %reduce-scatter.3.cloned.1.call-start = ((), (), s32[]{:S(2)}) async-start(), calls=%async_computation.3 | async-start | bytes 9437184 | tf_op jit(solution)/shard_map/reduce_scatter | solution.py:65
  10.5 30.6 %copy-start.3 = (f32[8,16]{1,0:T(8,128)S(1)}, f32[8,16]{1,0:T(8,128)}, u32[]{:S(2)}) copy-start(f32[8,16]{1,0:T(8,128)} %param.23) | copy-start | bytes 1540
  75.0 150.5 %copy-start = (bf16[256,1024]{1,0:T(8,128)(2,1)S(1)}, bf16[256,1024]{1,0:T(8,128)(2,1)}, u32[]{:S(2)}) copy-start(bf16[256,1024]{1,0:T(8,128)(2,1)} %param.16) | copy-start | bytes 1572868
  75.0 150.5 %copy-start.1 = (bf16[256,1024]{1,0:T(8,128)(2,1)S(1)}, bf16[256,1024]{1,0:T(8,128)(2,1)}, u32[]{:S(2)}) copy-start(bf16[256,1024]{1,0:T(8,128)(2,1)} %param.17) | copy-start | bytes 1572868
  75.0 155.6 %copy-start.4 = (f32[16,8]{0,1:T(8,128)S(1)}, f32[16,8]{0,1:T(8,128)}, u32[]{:S(2)}) copy-start(f32[16,8]{0,1:T(8,128)} %param.19) | copy-start | bytes 1540
  75.0 155.6 %copy-start.5 = (f32[16,8]{0,1:T(8,128)S(1)}, f32[16,8]{0,1:T(8,128)}, u32[]{:S(2)}) copy-start(f32[16,8]{0,1:T(8,128)} %param.21) | copy-start | bytes 1540
  75.0 226.0 %all-gather.8.cloned.1.call-start = ((), (), s32[]{:S(2)}) async-start(), calls=%async_computation.4 | async-start | bytes 4718592 | tf_op jit(solution)/shard_map/all_gather | solution.py:74
  228.5 147.0 %all-gather.10.cloned.1.call-start = ((), (), s32[]{:S(2)}) async-start(), calls=%async_computation.5 | async-start | bytes 4718592 | tf_op jit(solution)/shard_map/all_gather | solution.py:75
  229.0 175.8 %all-gather.12.cloned.1.call-start = ((), (), s32[]{:S(2)}) async-start(), calls=%async_computation.7 | async-start | bytes 12582912 | tf_op jit(solution)/shard_map/all_gather | solution.py:57
  229.6 242.8 %all-gather.14.cloned.1.call-start = ((), (), s32[]{:S(2)}) async-start(), calls=%async_computation.8 | async-start | bytes 4718592 | tf_op jit(solution)/shard_map/all_gather | solution.py:73
  230.2 269.2 %reduce-scatter.5.cloned.1.call-start = ((), (), s32[]{:S(2)}) async-start(), calls=%async_computation.6 | async-start | bytes 25165824 | tf_op jit(solution)/shard_map/reduce_scatter | solution.py:78
  301.0 2.2 copy-start.7
  402.0 0.8 copy-start.2
  404.9 9.0 %copy-start.6 = (bf16[2048,2048]{1,0:T(8,128)(2,1)S(1)}, bf16[2048,2048]{1,0:T(8,128)(2,1)}, u32[]{:S(2)}) copy-start(bf16[2048,2048]{1,0:T(8,128)(2,1)} %all-gather.12.cloned.1.call-done) | copy-start | bytes 25165828
  413.9 19.4 %copy-start.8 = (bf16[2048,1024]{1,0:T(8,128)(2,1)S(1)}, bf16[2048,1024]{1,0:T(8,128)(2,1)}, u32[]{:S(2)}) copy-start(bf16[2048,1024]{1,0:T(8,128)(2,1)} %all-gather.8.cloned.1.call-done) | copy-start | bytes 12582916
Sparse Core Ops, SparseCore 0:
  9.5 22.5 all-gather.5
  75.1 150.2 reduce-scatter.2
  228.6 72.3 all-gather.7
  303.8 71.6 all-gather.9
  376.9 18.1 all-gather.11
  397.9 74.5 all-gather.13
  474.8 24.5 reduce-scatter.4
where the time goes:
time: 521 us; the launch traced here: 513 us
  waiting for transfers between devices  326 us (63%)
  matrix products  130 us (25%)
  local copies, waits for them, and re-layouts  29.2 us (6%)
  between operations  14.4 us (3%)
  other arithmetic  9.08 us (2%)
    reduce_scatter x1, waiting for transfers between devices, local(): lax.psum_scatter(lax.dot_general(out_grad, down_full, inner, preferred_el...  150 us
    all_gather x1, waiting for transfers between devices, local(): lax.all_gather(gate_mine, 'row', axis=0, tiled=True)  70.3 us
    all_gather x1, waiting for transfers between devices, local(): lax.all_gather(up_mine, 'row', axis=0, tiled=True)  58.2 us
    dot_general x1, matrix products, local(): lax.dot_general(out_grad, down_full, inner, preferred_element_type=jnp.fl...  30 us
    dot_general x1, matrix products, local(): lax.dot_general(inputs, gate_grad, outer, preferred_element_type=jnp.floa...  26.1 us
    dot_general x1, matrix products, local(): lax.dot_general(up_grad, up_full, inner, preferred_element_type=jnp.float32)  22.7 us
    all_gather x1, waiting for transfers between devices, local(): lax.all_gather(grad_codes, 'col', axis=0, tiled=True)  21.6 us
    dot_general x1, matrix products, local(): lax.dot_general(inputs, up_grad, outer, preferred_element_type=jnp.float32)  19.4 us
  transfers between devices with their start and end apart: 7, of which 6 were waited for; matrix products, arithmetic and copies ran while one was open for 22% of the time, Pallas kernels for 0%

commit v1 on v0

v1 whole, which is shorter than its diff:
```python
import jax
import jax.numpy as jnp
from jax import lax
from jax.sharding import PartitionSpec as P

block_edge = 128
f32, bf16 = jnp.float32, jnp.bfloat16
inner = (((1,), (1,)), ((), ()))
outer = (((0,), (0,)), ((), ()))


def rows_dequant(codes, scale):
    count, width = codes.shape
    parts = codes.astype(f32).reshape(count, width // block_edge, block_edge)
    return (parts * scale.astype(f32)[:, :, None]).reshape(count, width).astype(bf16)


def tile_dequant(codes, scale):
    height, width = codes.shape
    parts = codes.astype(f32).reshape(
        height // block_edge, block_edge, width // block_edge, block_edge
    )
    return (parts * scale[:, None, :, None]).reshape(height, width).astype(bf16)


def dot(a, b, dims):
    return lax.dot_general(a, b, dims, preferred_element_type=f32)


def local(rows, *args):
    (
        x_codes,
        x_scale,
        grad_codes,
        grad_scale,
        gate_pre,
        up_pre,
        w_gate,
        gate_scale,
        w_up,
        up_scale,
        w_down,
        down_scale,
    ) = args
    line = rows // 2
    row = lax.axis_index("row")
    col = lax.axis_index("col")
    y, z = row % 2, row // 2
    swap_col = [(0, 1), (1, 0)]
    swap_y = [(i, i ^ 1) for i in range(rows)]

    def shift_z(k):
        return [(i, (i + 2 * k) % rows) for i in range(rows)]

    gate_all = lax.all_gather(gate_pre, "row", axis=0, tiled=True)
    up_all = lax.all_gather(up_pre, "row", axis=0, tiled=True)

    grad_own = rows_dequant(grad_codes, grad_scale)
    grad_other = lax.ppermute(grad_own, "col", swap_col)
    down_full = tile_dequant(w_down, down_scale)
    half = grad_own.shape[0]
    tokens = 2 * half
    chunk = tokens // rows
    units = down_full.shape[0]

    pieces = 2
    wide = units // pieces
    mine = []
    for j in range(pieces):
        down = down_full[j * wide : (j + 1) * wide]
        own = dot(grad_own, down, inner).reshape(line // 2, 2, chunk, wide)
        other = dot(grad_other, down, inner).reshape(line // 2, 2, chunk, wide)
        sums = []
        for part in (own, other):
            away = lax.dynamic_index_in_dim(part, 1 - y, 1, keepdims=False).astype(bf16)
            keep = lax.dynamic_index_in_dim(part, y, 1, keepdims=False)
            sums.append(keep + lax.ppermute(away, "row", swap_y).astype(f32))
        low = jnp.where(col == 0, sums[0], sums[1])
        high = jnp.where(col == 0, sums[1], sums[0])
        both = jnp.concatenate([low, high], axis=0)
        packed = both.astype(bf16)
        total = lax.dynamic_index_in_dim(both, z, 0, keepdims=False)
        for k in range(1, line):
            send = lax.dynamic_index_in_dim(packed, (z + k) % line, 0, keepdims=False)
            total = total + lax.ppermute(send, "row", shift_z(k)).astype(f32)
        mine.append(total.astype(bf16))
    hidden_grad = lax.all_gather(
        jnp.concatenate(mine, axis=1), "row", axis=0, tiled=True
    ).astype(f32)

    inputs = lax.all_gather(rows_dequant(x_codes, x_scale), "col", axis=0, tiled=True)
    out_grad = lax.all_gather(grad_own, "col", axis=0, tiled=True)
    factor = f32(1.0) / jnp.sqrt(f32(tokens))

    gate_val, up_val = gate_all.astype(f32), up_all.astype(f32)
    sigma = jax.nn.sigmoid(gate_val)
    active = gate_val * sigma
    hidden = (active * up_val).astype(bf16)
    slope = (up_val * sigma * (1.0 + gate_val * (1.0 - sigma))).astype(bf16)
    hidden, active, slope = lax.optimization_barrier((hidden, active.astype(bf16), slope))
    grad_down = (dot(hidden, out_grad, outer) * factor).astype(bf16)

    gate_grad = (hidden_grad * slope.astype(f32)).astype(bf16)
    up_grad = (hidden_grad * active.astype(f32)).astype(bf16)
    gate_grad, up_grad = lax.optimization_barrier((gate_grad, up_grad))
    gate_full = tile_dequant(w_gate, gate_scale)
    up_full = tile_dequant(w_up, up_scale)

    def input_part(which):
        gate = lax.dynamic_slice_in_dim(gate_grad, which * half, half, 0)
        up = lax.dynamic_slice_in_dim(up_grad, which * half, half, 0)
        return dot(gate, gate_full, inner) + dot(up, up_full, inner)

    away = input_part(1 - col).astype(bf16)
    back = lax.ppermute(away, "col", swap_col)
    grad_gate = (dot(inputs, gate_grad, outer) * factor).astype(bf16)
    grad_up = (dot(inputs, up_grad, outer) * factor).astype(bf16)
    grad_input = (input_part(col) + back.astype(f32)).astype(bf16)
    return (grad_input, grad_gate, grad_up, grad_down)


def solution(mesh):
    rows = mesh.shape["row"]
    return jax.shard_map(
        lambda *args: local(rows, *args),
        mesh=mesh,
        in_specs=(
            P(("grp", "col"), "row"),
            P(("grp", "col"), "row"),
            P(("grp", "col"), "row"),
            P(("grp", "col"), "row"),
            P(("grp", "row"), "col"),
            P(("grp", "row"), "col"),
            P("row", "col"),
            P("row", "col"),
            P("row", "col"),
            P("row", "col"),
            P("col", "row"),
            P("col", "row"),
        ),
        out_specs=(
            P(("grp", "col"), "row"),
            P(("grp", "row"), "col"),
            P(("grp", "row"), "col"),
            P(("grp", "col"), "row"),
        ),
        check_vma=False,
    )
```

time: 521 us -> 409 us (0.79)
  waiting for transfers between devices: 326 us -> 183 us
  starting transfers between devices: 0.53 us -> 36.8 us
  other arithmetic: 9.08 us -> 43.8 us
  matrix products: 130 us -> 105 us
  local copies, waits for them, and re-layouts: 29.2 us -> 21.6 us
    reduce_scatter x2 -> x0, waiting for transfers between devices: 160 us -> none  [the longest x1 150 us: local(): lax.psum_scatter(lax.dot_general(out_grad, down_full, inner, preferred_el...]
    ppermute x0 -> x12, waiting for transfers between devices: none -> 77.3 us  [the longest x4 41.9 us: local(): sums.append(keep + lax.ppermute(away, 'row', swap_y).astype(f32))]
    all_gather x5, waiting for transfers between devices: 163 us -> 104 us  [the longest x1 62.6 us: local(): lax.all_gather(jnp.concatenate(mine, axis=1), 'row', axis=0, tiled=True)]
    ppermute x0 -> x12, starting transfers between devices: none -> 36.4 us  [the longest x6 30.9 us: local(): total = total + lax.ppermute(send, 'row', shift_z(k)).astype(f32)]
    convert_element_type x2 -> x9, other arithmetic: 9.08 us -> 40.2 us  [the longest x1 11.4 us: local(): slope = (up_val * sigma * (1.0 + gate_val * (1.0 - sigma))).astype(bf16)]
    dot_general x6 -> x11, matrix products: 130 us -> 105 us  [dot(): return lax.dot_general(a, b, dims, preferred_element_type=f32)]
    mul x5, local copies, waits for them, and re-layouts: 26.3 us -> 6.44 us  [the longest x2 4.62 us: rows_dequant(): parts * scale.astype(f32)[:, :, None]]
    unnamed x20 -> x50, local copies, waits for them, and re-layouts: 2.48 us -> 12.2 us
  transfers between devices with their start and end apart: 7 -> 17, of which waited for: 6 -> 7; matrix products, arithmetic and copies ran while one was open for 22% -> 36% of each run, Pallas kernels for 0% -> 0%
where the time goes in v1:
time: 409 us; the launch traced here: 404 us
  waiting for transfers between devices  183 us (45%)
  matrix products  105 us (26%)
  other arithmetic  43.8 us (11%)
  starting transfers between devices  36.8 us (9%)
  local copies, waits for them, and re-layouts  21.6 us (5%)
  between operations  14.4 us (4%)
    dot_general x11, matrix products, dot(): return lax.dot_general(a, b, dims, preferred_element_type=f32)  105 us
    all_gather x1, waiting for transfers between devices, local(): lax.all_gather(jnp.concatenate(mine, axis=1), 'row', axis=0, tiled=True)  62.6 us
    ppermute x4, waiting for transfers between devices, local(): sums.append(keep + lax.ppermute(away, 'row', swap_y).astype(f32))  41.9 us
    ppermute x6, waiting for transfers between devices, local(): total = total + lax.ppermute(send, 'row', shift_z(k)).astype(f32)  35.4 us
    all_gather x1, waiting for transfers between devices, local(): gate_all = lax.all_gather(gate_pre, 'row', axis=0, tiled=True)  32.3 us
    ppermute x6, starting transfers between devices, local(): total = total + lax.ppermute(send, 'row', shift_z(k)).astype(f32)  30.9 us
    unnamed x50, local copies, waits for them, and re-layouts  12.2 us
    convert_element_type x1, other arithmetic, local(): slope = (up_val * sigma * (1.0 + gate_val * (1.0 - sigma))).astype(bf16)  11.4 us
  transfers between devices with their start and end apart: 17, of which 7 were waited for; matrix products, arithmetic and copies ran while one was open for 36% of the time, Pallas kernels for 0%

profile of v1, /device:TPU:0, one launch (start us, length us, event | category | flops | bytes accessed | tf_op | source)
XLA Modules:
  0.0 404.3 jit_solution(13081207333403912756)
XLA Ops:
  9.6 2.3 mul.96
  11.9 5.1 %fusion.13 = bf16[1024,2048]{1,0:T(8,128)(2,1)} fusion(f32[128,8,16,128]{3,2,1,0:T(8,128)S(1)} %bitcast.131, bf16[1024,2048]{1,0:T(8,128)(2,1)S(1)} %copy-done.7), kind=kLoop, calls=%fused_computation.25 | loop fusion | flops 6291456 | bytes 16777216 | tf_op jit(solution)/shard_map/convert_element_type | solution.py:15
  18.5 7.7 %fusion.12 = bf16[1024,2048]{1,0:T(8,128)(2,1)} fusion(f32[128,8,16,128]{3,2,1,0:T(8,128)S(1)} %bitcast.133, bf16[1024,2048]{1,0:T(8,128)(2,1)} %param.22), kind=kLoop, calls=%fused_computation.23 | loop fusion | flops 6291456 | bytes 16777216 | tf_op jit(solution)/shard_map/convert_element_type | solution.py:23
  26.2 4.1 %fusion.19 = f32[2,2,256,512]{3,2,1,0:T(8,128)S(1)} fusion(bf16[2,2,256,2048]{3,2,1,0:T(8,128)(2,1)S(1)} %bitcast.134, bf16[1024,2048]{1,0:T(8,128)(2,1)} %fusion.12), kind=kOutput, calls=%fused_computation.42 | convolution fusion | flops 2147483648 | bytes 8388608 | tf_op jit(solution)/shard_map/dot_general | solution.py:27
  31.6 2.9 collective-permute-start
  34.5 2.4 fusion.17
  38.5 5.4 %fusion.30 = f32[1024,512]{1,0:T(8,128)S(1)} fusion(bf16[1024,2048]{1,0:T(8,128)(2,1)} %collective-permute-done.1, bf16[1024,2048]{1,0:T(8,128)(2,1)} %fusion.12), kind=kOutput, calls=%fused_computation.53 | convolution fusion | flops 2147483648 | bytes 8388608 | tf_op jit(solution)/shard_map/dot_general | solution.py:27
  43.9 2.0 collective-permute-start.2
  45.9 5.4 %fusion.27 = f32[1024,512]{1,0:T(8,128)S(1)} fusion(bf16[1024,2048]{1,0:T(8,128)(2,1)} %collective-permute-done.1, bf16[1024,2048]{1,0:T(8,128)(2,1)S(1)} %copy-done.10), kind=kOutput, calls=%fused_computation.50 | convolution fusion | flops 2147483648 | bytes 8388608 | tf_op jit(solution)/shard_map/dot_general | solution.py:27
  52.3 39.4 %collective-permute-done.2 = bf16[2,256,512]{2,1,0:T(8,128)(2,1)S(1)} collective-permute-done((bf16[2,256,512]{2,1,0:T(8,128)(2,1)S(1)}, bf16[2,256,512]{2,1,0:T(8,128)(2,1)S(1)}, u32[]{:S(2)}, u32[]{:S(2)}) %collective-permute-start.2) | collective-permute-done | bytes 524320 | tf_op jit(solution)/shard_map/ppermute | solution.py:77
  95.7 2.7 collective-permute-start.4
  100.5 2.4 collective-permute-done.7
  106.3 3.8 collective-permute-start.10
  110.9 21.4 %collective-permute-start.9 = (bf16[256,512]{1,0:T(8,128)(2,1)}, bf16[256,512]{1,0:T(8,128)(2,1)}, u32[]{:S(2)}, u32[]{:S(2)}) collective-permute-start(bf16[256,512]{1,0:T(8,128)(2,1)} %get-tuple-element.28), channel_id=1, source_target_pairs={{0,8},{2,10},{4,12},{6,14},{8,0},{10,2},{12,4},{14,6},{1,9},{3,11}... | collective-permute-start | bytes 786440 | tf_op jit(solution)/shard_map/ppermute | solution.py:85
  133.6 4.5 %collective-permute-done.8 = bf16[256,512]{1,0:T(8,128)(2,1)} collective-permute-done((bf16[256,512]{1,0:T(8,128)(2,1)}, bf16[256,512]{1,0:T(8,128)(2,1)}, u32[]{:S(2)}, u32[]{:S(2)}) %collective-permute-start.8) | collective-permute-done | bytes 262176 | tf_op jit(solution)/shard_map/ppermute | solution.py:85
  138.2 30.9 %collective-permute-done.9 = bf16[256,512]{1,0:T(8,128)(2,1)} collective-permute-done((bf16[256,512]{1,0:T(8,128)(2,1)}, bf16[256,512]{1,0:T(8,128)(2,1)}, u32[]{:S(2)}, u32[]{:S(2)}) %collective-permute-start.9) | collective-permute-done | bytes 262176 | tf_op jit(solution)/shard_map/ppermute | solution.py:85
  171.6 2.3 mul.117
  174.3 5.2 %fusion.9 = bf16[1024,2048]{1,0:T(8,128)(2,1)} fusion(f32[128,8,16,128]{3,2,1,0:T(8,128)S(1)} %bitcast.132, bf16[1024,2048]{1,0:T(8,128)(2,1)S(1)} %copy-done.8), kind=kLoop, calls=%fused_computation.17 | loop fusion | flops 6291456 | bytes 16777216 | tf_op jit(solution)/shard_map/convert_element_type | solution.py:15
  180.3 32.3 %all-gather.8.cloned.1.call-done = bf16[2048,1024]{1,0:T(8,128)(2,1)} async-done(((bf16[256,1024]{1,0:T(8,128)(2,1)}), bf16[2048,1024]{1,0:T(8,128)(2,1)}) %all-gather.8.cloned.1.call-update) | async-done | bytes 4194320 | tf_op jit(solution)/shard_map/all_gather | solution.py:55
  212.6 11.4 %fusion.4 = (bf16[2048,1024]{1,0:T(8,128)(2,1)}, bf16[2048,1024]{1,0:T(8,128)(2,1)}, bf16[2048,1024]{1,0:T(8,128)(2,1)}) fusion(bf16[2048,1024]{1,0:T(8,128)(2,1)} %all-gather.10.cloned.1.call-done, bf16[2048,1024]{1,0:T(8,128)(2,1)} %all-gather.8.cloned.1.call-done), kind=kLoop, calls=%fused_computation.11 | loop fusion | flops 31457280 | bytes 20971520 | tf_op jit(solution)/shard_map/convert_element_type | solution.py:99
  224.0 8.9 %all-gather.14.cloned.1.call-done = bf16[2048,2048]{1,0:T(8,128)(2,1)} async-done(((bf16[1024,2048]{1,0:T(8,128)(2,1)}), bf16[2048,2048]{1,0:T(8,128)(2,1)}) %all-gather.14.cloned.1.call-update) | async-done | bytes 8388624 | tf_op jit(solution)/shard_map/all_gather | solution.py:92
  232.9 14.0 %multiply_convert_fusion = bf16[1024,2048]{1,0:T(8,128)(2,1)} fusion(bf16[2048,1024]{1,0:T(8,128)(2,1)} %get-tuple-element.13, bf16[2048,2048]{1,0:T(8,128)(2,1)} %all-gather.14.cloned.1.call-done), kind=kOutput, calls=%fused_computation.26 | convolution fusion | flops 8594128896 | bytes 16777216 | tf_op jit(solution)/shard_map/dot_general | solution.py:27
  246.9 62.6 %all-gather.6.cloned.1.call-done = bf16[2048,1024]{1,0:T(8,128)(2,1)} async-done(((bf16[256,1024]{1,0:T(8,128)(2,1)}), bf16[2048,1024]{1,0:T(8,128)(2,1)}) %all-gather.6.cloned.1.call-update) | async-done | bytes 4194320 | tf_op jit(solution)/shard_map/all_gather | solution.py:87
  309.5 7.7 %fusion.1 = (bf16[2048,1024]{1,0:T(8,128)(2,1)}, bf16[2048,1024]{1,0:T(8,128)(2,1)S(1)}) fusion(bf16[2048,1024]{1,0:T(8,128)(2,1)} %all-gather.6.cloned.1.call-done, bf16[2048,1024]{1,0:T(8,128)(2,1)} %get-tuple-element.10, bf16[2048,1024]{1,0:T(8,128)(2,1)} %get-tuple-element.9), kind=kLoop, calls=%fused_computation.8 | loop fusion | flops 14680064 | bytes 20971520 | tf_op jit(solution)/shard_map/convert_element_type | solution.py:104
  317.9 1.7 copy-done.5
  319.6 3.4 copy-done.23
  323.1 7.1 %fusion.22 = f32[1024,2048]{1,0:T(8,128)} fusion(bf16[2048,1024]{1,0:T(8,128)(2,1)S(1)} %get-tuple-element.11, s32[]{:T(128)S(6)} %select_n.105, f32[256,8,8,128]{3,2,1,0:T(8,128)S(1)} %bitcast.138, bf16[2048,1024]{1,0:T(8,128)(2,1)S(1)} %copy-done.23), kind=kOutput, calls=%fused_computation.45 | convolution fusion | flops 4301258752 | bytes 23068676 | tf_op jit(solution)/shard_map/dot_general | solution.py:27
  330.8 14.9 %add_convert_fusion.1 = bf16[1024,2048]{1,0:T(8,128)(2,1)} fusion(f32[1024,2048]{1,0:T(8,128)} %fusion.22, bf16[2048,1024]{1,0:T(8,128)(2,1)} %get-tuple-element.12, s32[]{:T(128)S(6)} %select_n.105, f32[256,8,8,128]{3,2,1,0:T(8,128)S(1)} %bitcast.136, bf16[2048,1024]{1,0:T(8,128)(2,1)} %param.20), kind=kOutput, calls=%fused_computation.30 | convolution fusion | flops 4305453056 | bytes 27262980 | tf_op jit(solution)/shard_map/dot_general | solution.py:27
  345.7 13.0 %fusion.25 = f32[1024,2048]{1,0:T(8,128)} fusion(bf16[2048,1024]{1,0:T(8,128)(2,1)} %copy-done.5, s32[]{:T(128)S(6)} %select_n.104, f32[256,8,8,128]{3,2,1,0:T(8,128)} %bitcast.139, bf16[2048,1024]{1,0:T(8,128)(2,1)} %param.18), kind=kOutput, calls=%fused_computation.48 | convolution fusion | flops 4301258752 | bytes 23068676 | tf_op jit(solution)/shard_map/dot_general | solution.py:27
  358.7 14.3 %multiply_convert_fusion.1 = bf16[2048,1024]{1,0:T(8,128)(2,1)} fusion(bf16[2048,2048]{1,0:T(8,128)(2,1)} %all-gather.12.cloned.1.call-done, bf16[2048,1024]{1,0:T(8,128)(2,1)} %get-tuple-element.12), kind=kOutput, calls=%fused_computation.27 | convolution fusion | flops 8594128896 | bytes 16777216 | tf_op jit(solution)/shard_map/dot_general | solution.py:27
  373.1 10.9 %multiply_convert_fusion.2 = bf16[2048,1024]{1,0:T(8,128)(2,1)} fusion(bf16[2048,2048]{1,0:T(8,128)(2,1)S(1)} %copy-done.22, bf16[2048,1024]{1,0:T(8,128)(2,1)S(1)} %copy-done.6), kind=kOutput, calls=%fused_computation.28 | convolution fusion | flops 8594128896 | bytes 16777216 | tf_op jit(solution)/shard_map/dot_general | solution.py:27
  384.0 13.6 %add_convert_fusion = bf16[1024,2048]{1,0:T(8,128)(2,1)} fusion(bf16[1024,2048]{1,0:T(8,128)(2,1)} %collective-permute-done.11, f32[1024,2048]{1,0:T(8,128)} %fusion.25, bf16[2048,1024]{1,0:T(8,128)(2,1)S(1)} %copy-done.4, s32[]{:T(128)S(6)} %select_n.104, f32[256,8,8,128]{3,2,1,0:T(8,128)} %bitcast.137, bf16[2048,1024]{1,0:T(8,128)(2,1)} %param.20), kind=kOutput, calls=%fused_computation.29 | convolution fusion | flops 4309647360 | bytes 31457284 | tf_op jit(solution)/shard_map/dot_general | solution.py:27
  (93 shorter events, 23.9 us)
Async XLA Ops:
  7.2 173.1 %all-gather.10.cloned.1.call-start = ((), (), s32[]{:S(2)}) async-start(), calls=%async_computation.2 | async-start | bytes 4718592 | tf_op jit(solution)/shard_map/all_gather | solution.py:56
  7.9 204.7 %all-gather.8.cloned.1.call-start = ((), (), s32[]{:S(2)}) async-start(), calls=%async_computation.1 | async-start | bytes 4718592 | tf_op jit(solution)/shard_map/all_gather | solution.py:55
  8.6 224.3 %all-gather.14.cloned.1.call-start = ((), (), s32[]{:S(2)}) async-start(), calls=%async_computation.4 | async-start | bytes 12582912 | tf_op jit(solution)/shard_map/all_gather | solution.py:92
  9.6 2.3 copy-start.7
  17.1 292.4 %all-gather.6.cloned.1.call-start = ((), (), s32[]{:S(2)}) async-start(), calls=%async_computation | async-start | bytes 4718592 | tf_op jit(solution)/shard_map/all_gather | solution.py:87
  17.3 21.1 %collective-permute-start.1 = (bf16[1024,2048]{1,0:T(8,128)(2,1)}, bf16[1024,2048]{1,0:T(8,128)(2,1)}, u32[]{:S(2)}, u32[]{:S(2)}) collective-permute-start(bf16[1024,2048]{1,0:T(8,128)(2,1)} %fusion.13), channel_id=1, source_target_pairs={{0,1},{1,0},{2,3},{3,2},{4,5},{5,4},{6,7},{7,6},{8,9},{9,8},{10,11... | collective-permute-start | bytes 12582920 | tf_op jit(solution)/shard_map/ppermute | solution.py:59
  18.4 7.7 %copy-start = (bf16[1024,2048]{1,0:T(8,128)(2,1)S(1)}, bf16[1024,2048]{1,0:T(8,128)(2,1)}, u32[]{:S(2)}) copy-start(bf16[1024,2048]{1,0:T(8,128)(2,1)} %fusion.13) | copy-start | bytes 12582916
  26.2 8.3 %copy-start.9 = (bf16[1024,2048]{1,0:T(8,128)(2,1)S(1)}, bf16[1024,2048]{1,0:T(8,128)(2,1)}, u32[]{:S(2)}) copy-start(bf16[1024,2048]{1,0:T(8,128)(2,1)} %fusion.12) | copy-start | bytes 12582916
  31.6 19.9 %collective-permute-start = (bf16[2,256,512]{2,1,0:T(8,128)(2,1)S(1)}, bf16[2,256,512]{2,1,0:T(8,128)(2,1)S(1)}, u32[]{:S(2)}, u32[]{:S(2)}) collective-permute-start(bf16[2,256,512]{2,1,0:T(8,128)(2,1)S(1)} %fusion.37), channel_id=1, source_target_pairs={{0,2},{2,0},{4,6},{6,4},{8,10},{10,8},{12,14},{14,12},{1,3},{3,1},... | collective-permute-start | bytes 1572872 | tf_op jit(solution)/shard_map/ppermute | solution.py:77
  38.3 61.4 %collective-permute-start.6 = (bf16[2,256,512]{2,1,0:T(8,128)(2,1)S(1)}, bf16[2,256,512]{2,1,0:T(8,128)(2,1)S(1)}, u32[]{:S(2)}, u32[]{:S(2)}) collective-permute-start(bf16[2,256,512]{2,1,0:T(8,128)(2,1)S(1)} %fusion.39), channel_id=1, source_target_pairs={{0,2},{2,0},{4,6},{6,4},{8,10},{10,8},{12,14},{14,12},{1,3},{3,1},... | collective-permute-start | bytes 1572872 | tf_op jit(solution)/shard_map/ppermute | solution.py:77
  38.4 7.5 %copy-start.10 = (bf16[1024,2048]{1,0:T(8,128)(2,1)S(1)}, bf16[1024,2048]{1,0:T(8,128)(2,1)}, u32[]{:S(2)}) copy-start(bf16[1024,2048]{1,0:T(8,128)(2,1)} %fusion.12) | copy-start | bytes 12582916
  43.9 47.8 %copy-start.14 = (f32[2,2,256,512]{3,2,1,0:T(8,128)S(1)}, f32[2,2,256,512]{3,2,1,0:T(8,128)}, u32[]{:S(2)}) copy-start(f32[2,2,256,512]{3,2,1,0:T(8,128)} %copy-done.13) | copy-start | bytes 6291460
  43.9 47.8 %collective-permute-start.2 = (bf16[2,256,512]{2,1,0:T(8,128)(2,1)S(1)}, bf16[2,256,512]{2,1,0:T(8,128)(2,1)S(1)}, u32[]{:S(2)}, u32[]{:S(2)}) collective-permute-start(bf16[2,256,512]{2,1,0:T(8,128)(2,1)S(1)} %fusion.38), channel_id=1, source_target_pairs={{0,2},{2,0},{4,6},{6,4},{8,10},{10,8},{12,14},{14,12},{1,3},{3,1},... | collective-permute-start | bytes 1572872 | tf_op jit(solution)/shard_map/ppermute | solution.py:77
  51.4 51.5 %copy-start.12 = (f32[2,2,256,512]{3,2,1,0:T(8,128)S(1)}, f32[2,2,256,512]{3,2,1,0:T(8,128)}, u32[]{:S(2)}) copy-start(f32[2,2,256,512]{3,2,1,0:T(8,128)} %copy-done.11) | copy-start | bytes 6291460
  51.4 51.5 %collective-permute-start.7 = (bf16[2,256,512]{2,1,0:T(8,128)(2,1)S(1)}, bf16[2,256,512]{2,1,0:T(8,128)(2,1)S(1)}, u32[]{:S(2)}, u32[]{:S(2)}) collective-permute-start(bf16[2,256,512]{2,1,0:T(8,128)(2,1)S(1)} %fusion.40), channel_id=1, source_target_pairs={{0,2},{2,0},{4,6},{6,4},{8,10},{10,8},{12,14},{14,12},{1,3},{3,1},... | collective-permute-start | bytes 1572872 | tf_op jit(solution)/shard_map/ppermute | solution.py:77
  94.1 16.1 %collective-permute-start.3 = (bf16[256,512]{1,0:T(8,128)(2,1)S(1)}, bf16[256,512]{1,0:T(8,128)(2,1)S(1)}, u32[]{:S(2)}, u32[]{:S(2)}) collective-permute-start(bf16[256,512]{1,0:T(8,128)(2,1)S(1)} %get-tuple-element.23), channel_id=1, source_target_pairs={{0,4},{2,6},{4,8},{6,10},{8,12},{10,14},{12,0},{14,2},{1,5},{3,7},... | collective-permute-start | bytes 786440 | tf_op jit(solution)/shard_map/ppermute | solution.py:85
  95.7 36.6 %collective-permute-start.4 = (bf16[256,512]{1,0:T(8,128)(2,1)}, bf16[256,512]{1,0:T(8,128)(2,1)}, u32[]{:S(2)}, u32[]{:S(2)}) collective-permute-start(bf16[256,512]{1,0:T(8,128)(2,1)} %get-tuple-element.25), channel_id=1, source_target_pairs={{0,8},{2,10},{4,12},{6,14},{8,0},{10,2},{12,4},{14,6},{1,9},{3,11}... | collective-permute-start | bytes 786440 | tf_op jit(solution)/shard_map/ppermute | solution.py:85
  98.5 33.8 %collective-permute-start.5 = (bf16[256,512]{1,0:T(8,128)(2,1)S(1)}, bf16[256,512]{1,0:T(8,128)(2,1)}, u32[]{:S(2)}, u32[]{:S(2)}) collective-permute-start(bf16[256,512]{1,0:T(8,128)(2,1)S(1)} %get-tuple-element.24), channel_id=1, source_target_pairs={{0,12},{2,14},{4,0},{6,2},{8,4},{10,6},{12,8},{14,10},{1,13},{3,15... | collective-permute-start | bytes 786440 | tf_op jit(solution)/shard_map/ppermute | solution.py:85
  106.3 65.1 %copy-start.18 = (bf16[1024,16]{0,1:T(8,128)(2,1)S(1)}, bf16[1024,16]{0,1:T(8,128)(2,1)}, u32[]{:S(2)}) copy-start(bf16[1024,16]{0,1:T(8,128)(2,1)} %param.13) | copy-start | bytes 98308
  106.3 27.3 %collective-permute-start.10 = (bf16[256,512]{1,0:T(8,128)(2,1)}, bf16[256,512]{1,0:T(8,128)(2,1)}, u32[]{:S(2)}, u32[]{:S(2)}) collective-permute-start(bf16[256,512]{1,0:T(8,128)(2,1)} %get-tuple-element.27), channel_id=1, source_target_pairs={{0,12},{2,14},{4,0},{6,2},{8,4},{10,6},{12,8},{14,10},{1,13},{3,15... | collective-permute-start | bytes 786440 | tf_op jit(solution)/shard_map/ppermute | solution.py:85
  110.2 28.0 %collective-permute-start.8 = (bf16[256,512]{1,0:T(8,128)(2,1)}, bf16[256,512]{1,0:T(8,128)(2,1)}, u32[]{:S(2)}, u32[]{:S(2)}) collective-permute-start(bf16[256,512]{1,0:T(8,128)(2,1)} %get-tuple-element.26), channel_id=1, source_target_pairs={{0,4},{2,6},{4,8},{6,10},{8,12},{10,14},{12,0},{14,2},{1,5},{3,7},... | collective-permute-start | bytes 786440 | tf_op jit(solution)/shard_map/ppermute | solution.py:85
  110.9 58.2 %collective-permute-start.9 = (bf16[256,512]{1,0:T(8,128)(2,1)}, bf16[256,512]{1,0:T(8,128)(2,1)}, u32[]{:S(2)}, u32[]{:S(2)}) collective-permute-start(bf16[256,512]{1,0:T(8,128)(2,1)} %get-tuple-element.28), channel_id=1, source_target_pairs={{0,8},{2,10},{4,12},{6,14},{8,0},{10,2},{12,4},{14,6},{1,9},{3,11}... | collective-permute-start | bytes 786440 | tf_op jit(solution)/shard_map/ppermute | solution.py:85
  171.4 187.3 %all-gather.12.cloned.1.call-start = ((), (), s32[]{:S(2)}) async-start(), calls=%async_computation.3 | async-start | bytes 12582912 | tf_op jit(solution)/shard_map/all_gather | solution.py:91
  171.6 2.7 copy-start.8
  317.2 2.4 copy-start.5
  317.2 5.8 %copy-start.23 = (bf16[2048,1024]{1,0:T(8,128)(2,1)S(1)}, bf16[2048,1024]{1,0:T(8,128)(2,1)}, u32[]{:S(2)}) copy-start(bf16[2048,1024]{1,0:T(8,128)(2,1)} %param.18) | copy-start | bytes 12582916
  317.9 12.3 %copy-start.3 = (f32[16,128,8,128]{3,2,1,0:T(8,128)}, f32[16,128,8,128]{3,2,1,0:T(8,128)S(1)}, u32[]{:S(2)}) copy-start(f32[16,128,8,128]{3,2,1,0:T(8,128)S(1)} %mul.110) | copy-start | bytes 25165828
  330.8 14.9 %copy-start.2 = (f32[16,128,8,128]{3,2,1,0:T(8,128)}, f32[16,128,8,128]{3,2,1,0:T(8,128)S(1)}, u32[]{:S(2)}) copy-start(f32[16,128,8,128]{3,2,1,0:T(8,128)S(1)} %mul.113) | copy-start | bytes 25165828
  345.7 38.3 %collective-permute-start.11 = (bf16[1024,2048]{1,0:T(8,128)(2,1)}, bf16[1024,2048]{1,0:T(8,128)(2,1)}, u32[]{:S(2)}, u32[]{:S(2)}) collective-permute-start(bf16[1024,2048]{1,0:T(8,128)(2,1)} %add_convert_fusion.1), channel_id=1, source_target_pairs={{0,1},{1,0},{2,3},{3,2},{4,5},{5,4},{6,7},{7,6},{8,9},{9,8},{10,11... | collective-permute-start | bytes 12582920 | tf_op jit(solution)/shard_map/ppermute | solution.py:115
  358.7 14.3 %copy-start.6 = (bf16[2048,1024]{1,0:T(8,128)(2,1)S(1)}, bf16[2048,1024]{1,0:T(8,128)(2,1)}, u32[]{:S(2)}) copy-start(bf16[2048,1024]{1,0:T(8,128)(2,1)} %copy-done.5) | copy-start | bytes 12582916
  358.7 14.3 %copy-start.22 = (bf16[2048,2048]{1,0:T(8,128)(2,1)S(1)}, bf16[2048,2048]{1,0:T(8,128)(2,1)}, u32[]{:S(2)}) copy-start(bf16[2048,2048]{1,0:T(8,128)(2,1)} %all-gather.12.cloned.1.call-done) | copy-start | bytes 25165828
  373.1 10.9 %copy-start.4 = (bf16[2048,1024]{1,0:T(8,128)(2,1)S(1)}, bf16[2048,1024]{1,0:T(8,128)(2,1)}, u32[]{:S(2)}) copy-start(bf16[2048,1024]{1,0:T(8,128)(2,1)} %get-tuple-element.12) | copy-start | bytes 12582916
  (9 other events, 8.1 us)
Sparse Core Ops, SparseCore 0:
  10.1 114.4 all-gather.9
  126.7 85.8 all-gather.7
  214.7 18.1 all-gather.13
  234.9 74.5 all-gather.5
  310.9 18.1 all-gather.11
